TPU v7x, 32 devices: a whole 2x2x4 slice. The times are simulated.
32 devices in a mesh: groups: 2 (over y), ctx: 8 (over z, x), head: 2 (over core).
Axes of the slice: x: 2, y: 2, z: 4, core: 2. Of those that a mesh axis runs over, the one named last changes fastest.
Arguments:
- hist_x: bfloat16 [4096, 1024], P(('groups', 'ctx')), parts along dimension 0, may hold values from -6 to 6
- cand_x: bfloat16 [64, 1024], P(('groups', 'ctx')), parts along dimension 0, may hold values from -6 to 6
- w_qkv: bfloat16 [3, 1024, 1024], P(None, None, 'head'), may hold values from -0.1875 to 0.1875
- rab_table: float32 [128, 8], P(None, 'head'), may hold values from -2 to 2
- hist_len: int32 [16], P(('groups', 'ctx')), parts along dimension 0, may hold values from 64 to 256, as said below
- hist_bucket: int32 [4096], P(('groups', 'ctx')), parts along dimension 0, may hold values from 0 to 127
- cand_owner: int32 [64], P('groups'), parts along dimension 0, may hold values from 0 to 31, each once
Outputs:
- hist_out: bfloat16 [4096, 1024], P(('groups', 'ctx'), 'head'), parts along dimension 0
- cand_out: bfloat16 [64, 1024], P(('groups', 'ctx'), 'head'), parts along dimension 0
There are 2 independent parts, one for each index of `groups`. A program takes and returns all parts, laid end to end along the dimension named above; an argument that names none is the same for every part. Nothing has to cross between parts.
Inputs may be any that keep to these rules, and one draw needn't show every extreme that they name: `hist_len`: every index of ctx holds at least a quarter of its 256 events valid, and one index is full in every draw. `cand_owner`: each of 0 to 31 appears once.
All inputs are finite; a program needn't handle non-finite values.
Results may differ from a plain program's by a relative error of at most 0.0085.
Values may be sent and summed in bfloat16 or wider, within the bound.
A program may use at most 64 MiB of HBM per device.

v0:
```python
import math

import jax
import jax.numpy as jnp
from jax import lax
from jax.sharding import PartitionSpec as P

WINDOW = 256


def from_behind(value, axis, steps):
    count = lax.axis_size(axis)
    leading, last = (max(0, -steps), min(count, count - steps))
    return lax.ppermute(value, axis, [(source, source + steps) for source in range(leading, last)])


def local(hist_x, cand_x, w_qkv, rab_table, hist_len, hist_bucket, cand_owner):
    row_count = hist_x.shape[0]
    width_part = w_qkv.shape[2]
    head_count = rab_table.shape[1]
    head_size = width_part // head_count
    score_scale = head_size ** (-0.5)
    queries = jnp.dot(hist_x, w_qkv[0], preferred_element_type=jnp.float32).astype(jnp.bfloat16)
    key_rows = jnp.dot(hist_x, w_qkv[1], preferred_element_type=jnp.float32).astype(jnp.bfloat16)
    raw_values = jnp.dot(hist_x, w_qkv[2], preferred_element_type=jnp.float32).astype(jnp.bfloat16)
    is_valid = jnp.arange(row_count, dtype=jnp.int32)[:, None] < hist_len[0]
    values = jnp.where(is_valid, raw_values, jnp.zeros((), jnp.bfloat16))
    bucket_hot = (
        hist_bucket[:, None] == jnp.arange(rab_table.shape[0], dtype=jnp.int32)[None, :]
    ).astype(jnp.float32)
    key_bias = jnp.einsum(
        "nh,rn->hr", rab_table, bucket_hot, precision=lax.Precision.HIGHEST
    ).astype(jnp.bfloat16)
    edge_keys, edge_values, edge_bias = from_behind((key_rows, values, key_bias), "ctx", 1)
    keys_joined = jnp.concatenate([edge_keys, key_rows], 0)
    values_joined = jnp.concatenate([edge_values, values], 0)
    bias_joined = jnp.concatenate([edge_bias, key_bias], 1)
    block_rows = math.gcd(row_count, 512)
    span_rows = block_rows + WINDOW
    distance = (
        jnp.arange(block_rows, dtype=jnp.int32)[:, None]
        + WINDOW
        - jnp.arange(span_rows, dtype=jnp.int32)[None, :]
    )
    in_window = (distance >= 0) & (distance < WINDOW)

    def window_block(first_row):
        q_block = queries.reshape(block_rows, head_count, head_size)
        k_block = keys_joined.reshape(span_rows, head_count, head_size)
        v_block = values_joined.reshape(span_rows, head_count, head_size)
        b_block = bias_joined.astype(jnp.float32)
        scores = (
            jnp.einsum("qhd,khd->hqk", q_block, k_block, preferred_element_type=jnp.float32)
            * score_scale
            + b_block[:, None, :]
        )
        weights = jnp.where(in_window[None], jax.nn.silu(scores), 0.0).astype(jnp.bfloat16)
        return jnp.einsum(
            "hqk,khd->qhd", weights, v_block, preferred_element_type=jnp.float32
        ).reshape(block_rows, width_part)

    block_starts = jnp.arange(row_count // block_rows, dtype=jnp.int32) * block_rows
    hist_sum = lax.map(window_block, block_starts).reshape(row_count, width_part)
    hist_out = jnp.where(is_valid, hist_sum * WINDOW ** (-0.5), 0.0).astype(jnp.bfloat16)
    own_query = jnp.dot(cand_x, w_qkv[0], preferred_element_type=jnp.float32).astype(jnp.bfloat16)
    all_query = lax.all_gather(own_query, "ctx", axis=0, tiled=True)
    cand_total = all_query.shape[0]
    inverse = (
        jnp.zeros((cand_total,), jnp.int32)
        .at[cand_owner]
        .set(jnp.arange(cand_total, dtype=jnp.int32))
    )
    ordered = jnp.take(all_query, inverse, axis=0)
    keys_heads = key_rows.reshape(row_count, head_count, head_size)
    values_by_head = jnp.transpose(values.reshape(row_count, head_count, head_size), (1, 2, 0))
    bias_float = key_bias.astype(jnp.float32)
    norm_scale = (row_count * lax.axis_size("ctx")) ** (-0.5)
    piece_rows = math.gcd(cand_total, 256)

    def one_block(offset):
        q_block = lax.dynamic_slice_in_dim(ordered, 0 + offset, piece_rows, 0).reshape(
            piece_rows, head_count, head_size
        )
        scores = (
            jnp.einsum("khd,chd->hkc", keys_heads, q_block, preferred_element_type=jnp.float32)
            * score_scale
            + bias_float[:, :, None]
        )
        weights = jax.nn.silu(scores).astype(jnp.bfloat16)
        summed = jnp.einsum(
            "hdk,hkc->chd", values_by_head, weights, preferred_element_type=jnp.float32
        )
        return summed.reshape(piece_rows, width_part) * norm_scale

    pieces = lax.map(one_block, jnp.arange(cand_total // piece_rows, dtype=jnp.int32) * piece_rows)
    cand_sum = lax.psum_scatter(
        pieces.reshape(cand_total, width_part), "ctx", scatter_dimension=0, tiled=True
    )
    return (hist_out, cand_sum.astype(jnp.bfloat16))


def solution(mesh):
    placed = (
        P(("groups", "ctx"), None),
        P(("groups", "ctx"), None),
        P(None, None, "head"),
        P(None, "head"),
        P(("groups", "ctx")),
        P(("groups", "ctx")),
        P("groups"),
    )
    return jax.shard_map(
        local,
        mesh=mesh,
        in_specs=placed,
        out_specs=(P(("groups", "ctx"), "head"), P(("groups", "ctx"), "head")),
        check_vma=False,
    )
```

profile of v0, /device:TPU:0, one launch (start us, length us, event | category | flops | bytes accessed | tf_op | source)
XLA Modules:
  0.0 92.2 jit_solution(2179853245009059249)
XLA Ops:
  0.6 0.0 copy-start
  0.6 0.9 %fusion.53 = (f32[4,256]{1,0:T(4,128)S(1)}, bf16[4,256]{1,0:T(4,128)(2,1)S(1)}) fusion(f32[128,4]{0,1:T(4,128)} %param.10, s32[256]{0:T(256)} %param.12), kind=kOutput, calls=%fused_computation.67 | convolution fusion | flops 1607680 | bytes 9216 | tf_op jit(solution)/shard_map/nh,rn->hr/dot_general | solution.py:31
  1.6 0.0 copy-start.2
  1.6 5.0 %collective-permute-start.2 = (bf16[4,256]{1,0:T(4,128)(2,1)S(1)}, bf16[4,256]{1,0:T(4,128)(2,1)S(1)}, u32[]{:S(2)}, u32[]{:S(2)}) collective-permute-start(bf16[4,256]{1,0:T(4,128)(2,1)S(1)} %get-tuple-element.30), channel_id=1, source_target_pairs={{0,2},{2,4},{4,6},{6,8},{8,10},{10,12},{12,14},{1,3},{3,5},{5,7},{... | collective-permute-start | bytes 6152 | tf_op jit(solution)/shard_map/ppermute | solution.py:14
  6.6 0.0 copy-done
  6.6 1.7 %convolution_convert_fusion = bf16[256,512]{1,0:T(8,128)(2,1)S(1)} fusion(bf16[256,1024]{1,0:T(8,128)(2,1)S(1)} %copy-done, bf16[3,1024,512]{2,1,0:T(8,128)(2,1)} %param.9), kind=kOutput, calls=%fused_computation.4 | convolution fusion | flops 268566528 | bytes 1835008 | tf_op jit(solution)/shard_map/dot_general | solution.py:24
  8.3 3.5 %collective-permute-start.1 = (bf16[256,512]{1,0:T(8,128)(2,1)S(1)}, bf16[256,512]{1,0:T(8,128)(2,1)S(1)}, u32[]{:S(2)}, u32[]{:S(2)}) collective-permute-start(bf16[256,512]{1,0:T(8,128)(2,1)S(1)} %convolution_convert_fusion), channel_id=1, source_target_pairs={{0,2},{2,4},{4,6},{6,8},{8,10},{10,12},{12,14},{1,3},{3,5},{5,7},{... | collective-permute-start | bytes 786440 | tf_op jit(solution)/shard_map/ppermute | solution.py:14
  12.4 0.0 copy-start.1
  12.5 1.7 %fusion = bf16[256,512]{1,0:T(8,128)(2,1)S(1)} fusion(bf16[256,1024]{1,0:T(8,128)(2,1)S(1)} %copy-done, bf16[3,1024,512]{2,1,0:T(8,128)(2,1)} %param.9, pred[256]{0:T(512)(128)(4,1)S(1)} %iota_compare_fusion.2), kind=kOutput, calls=%fused_computation.7 | convolution fusion | flops 268697600 | bytes 1835264 | tf_op jit(solution)/shard_map/dot_general | solution.py:25
  14.1 3.4 %collective-permute-start = (bf16[256,512]{1,0:T(8,128)(2,1)S(1)}, bf16[256,512]{1,0:T(8,128)(2,1)S(1)}, u32[]{:S(2)}, u32[]{:S(2)}) collective-permute-start(bf16[256,512]{1,0:T(8,128)(2,1)S(1)} %fusion), channel_id=1, source_target_pairs={{0,2},{2,4},{4,6},{6,8},{8,10},{10,12},{12,14},{1,3},{3,5},{5,7},{... | collective-permute-start | bytes 786440 | tf_op jit(solution)/shard_map/ppermute | solution.py:14
  17.5 0.0 copy-done.2
  17.6 0.7 scatter_custom_fusion
  18.3 0.1 copy.34
  18.4 0.0 copy-start.3
  18.4 1.7 %fusion.1 = bf16[32,4,8,128]{3,2,1,0:T(8,128)(2,1)S(1)} fusion(bf16[256,1024]{1,0:T(8,128)(2,1)S(1)} %copy-done, bf16[3,1024,512]{2,1,0:T(8,128)(2,1)} %param.9), kind=kOutput, calls=%fused_computation.8 | convolution fusion | flops 268566528 | bytes 1835008 | tf_op jit(solution)/shard_map/dot_general | solution.py:23
  20.1 0.0 copy-done.1
  20.1 1.5 %fusion.4 = bf16[1,4,512]{2,1,0:T(4,128)(2,1)S(1)} fusion(bf16[4,1024]{1,0:T(4,128)(2,1)S(1)} %copy-done.1, bf16[3,1024,512]{2,1,0:T(8,128)(2,1)} %param.9), kind=kOutput, calls=%fused_computation.14 | convolution fusion | flops 4196352 | bytes 1060864 | tf_op jit(solution)/shard_map/dot_general | solution.py:65
  21.6 30.4 %all-gather = bf16[8,4,512]{2,1,0:T(4,128)(2,1)S(1)} all-gather(bf16[1,4,512]{2,1,0:T(4,128)(2,1)S(1)} %fusion.4), channel_id=1, replica_groups=mesh['groups'=2,'ctx'=8,'head'=2] {'ctx'}, dimensions={0}, use_global_device_ids=true | all-gather | bytes 36864 | tf_op jit(solution)/shard_map/all_gather | solution.py:66
  52.0 0.2 fusion.23
  52.2 0.6 gather_fusion
  52.9 0.4 fusion.3
  53.2 0.0 copy-done.3
  53.3 0.6 dynamic-slice
  54.5 34.8 %all-reduce = bf16[32,512]{1,0:T(8,128)(2,1)S(1)} all-reduce(f32[32,512]{1,0:T(8,128)S(1)} %bitcast.78), channel_id=2, replica_groups=mesh['groups'=2,'ctx'=8,'head'=2] {'ctx'}, use_global_device_ids=true, to_apply=%region_1.2.clone | all-reduce | flops 16384 | bytes 98304
  89.3 0.6 dynamic-slice_convert_fusion
  89.9 0.0 collective-permute-done.2
  89.9 0.0 collective-permute-done
  90.0 0.2 copy.32
  90.2 0.0 collective-permute-done.1
  90.2 1.0 %convolution_multiply_fusion = bf16[4,128,256]{2,1,0:T(8,128)(2,1)S(1)} fusion(bf16[512,4,128]{0,2,1:T(8,128)(2,1)S(1)} %bitcast.75, f32[4,512]{1,0:T(4,128)S(1)} %maximum_convert_fusion, pred[256,512]{1,0:T(8,128)(4,1)S(1)} %fusion.23, bf16[32,4,8,128]{3,2,1,0:T(8,128)(2,1)S(1)} %fusion.1, bf16[256,512]{1,0:T(8,128)(2,1)S(1)} %convolution_convert_fusion, ...), kind=kOutput, calls=%fused_computation.3 | convolution fusion | flops 273940480 | bytes 1712128 | tf_op jit(solution)/shard_map/while/body/eval_jaxpr/hqk,khd->qhd/dot_general | solution.py:58
  91.3 0.1 copy.33
  91.4 0.8 select_convert_fusion.2
  (11 shorter events, 0.1 us)
Async XLA Ops:
  0.6 6.0 %copy-start = (bf16[256,1024]{1,0:T(8,128)(2,1)S(1)}, bf16[256,1024]{1,0:T(8,128)(2,1)}, u32[]{:S(2)}) copy-start(bf16[256,1024]{1,0:T(8,128)(2,1)} %param.7) | copy-start | bytes 1572868
  1.6 16.0 %copy-start.2 = (s32[32]{0:T(128)S(1)}, s32[32]{0:T(128)}, u32[]{:S(2)}) copy-start(s32[32]{0:T(128)} %param.13) | copy-start | bytes 388
  1.6 88.3 %collective-permute-start.2 = (bf16[4,256]{1,0:T(4,128)(2,1)S(1)}, bf16[4,256]{1,0:T(4,128)(2,1)S(1)}, u32[]{:S(2)}, u32[]{:S(2)}) collective-permute-start(bf16[4,256]{1,0:T(4,128)(2,1)S(1)} %get-tuple-element.30), channel_id=1, source_target_pairs={{0,2},{2,4},{4,6},{6,8},{8,10},{10,12},{12,14},{1,3},{3,5},{5,7},{... | collective-permute-start | bytes 6152 | tf_op jit(solution)/shard_map/ppermute | solution.py:14
  8.3 81.9 %collective-permute-start.1 = (bf16[256,512]{1,0:T(8,128)(2,1)S(1)}, bf16[256,512]{1,0:T(8,128)(2,1)S(1)}, u32[]{:S(2)}, u32[]{:S(2)}) collective-permute-start(bf16[256,512]{1,0:T(8,128)(2,1)S(1)} %convolution_convert_fusion), channel_id=1, source_target_pairs={{0,2},{2,4},{4,6},{6,8},{8,10},{10,12},{12,14},{1,3},{3,5},{5,7},{... | collective-permute-start | bytes 786440 | tf_op jit(solution)/shard_map/ppermute | solution.py:14
  12.4 7.7 %copy-start.1 = (bf16[4,1024]{1,0:T(4,128)(2,1)S(1)}, bf16[4,1024]{1,0:T(4,128)(2,1)}, u32[]{:S(2)}) copy-start(bf16[4,1024]{1,0:T(4,128)(2,1)} %param.8) | copy-start | bytes 24580
  14.1 75.8 %collective-permute-start = (bf16[256,512]{1,0:T(8,128)(2,1)S(1)}, bf16[256,512]{1,0:T(8,128)(2,1)S(1)}, u32[]{:S(2)}, u32[]{:S(2)}) collective-permute-start(bf16[256,512]{1,0:T(8,128)(2,1)S(1)} %fusion), channel_id=1, source_target_pairs={{0,2},{2,4},{4,6},{6,8},{8,10},{10,12},{12,14},{1,3},{3,5},{5,7},{... | collective-permute-start | bytes 786440 | tf_op jit(solution)/shard_map/ppermute | solution.py:14
  18.4 34.8 %copy-start.3 = (u32[32]{0:T(128)S(1)}, u32[32]{0:T(128)}, u32[]{:S(2)}) copy-start(u32[32]{0:T(128)} %constant.69) | copy-start | bytes 388
where the time goes:
time: 92.6 us; the launch traced here: 92.2 us
  blocking collectives  65.2 us (70%)
  starting transfers between devices  11.9 us (13%)
  matrix products  8.81 us (10%)
  local copies, waits for them, and re-layouts  3.02 us (3%)
  between operations  2.17 us (2%)
  other arithmetic  1.08 us (1%)
    unnamed x1, blocking collectives  34.8 us
    all_gather x1, blocking collectives, local(): all_query = lax.all_gather(own_query, 'ctx', axis=0, tiled=True)  30.4 us
    ppermute x3, starting transfers between devices, from_behind(): lax.ppermute(value, axis, [(source, source + steps) for source in range(l...  11.9 us
  transfers between devices with their start and end apart: 3, of which 0 were waited for; matrix products, arithmetic and copies ran while one was open for 11% of the time, Pallas kernels for 0%

commit v1 on v0

v1 whole, which is shorter than its diff:
```python
import functools

import jax
import jax.numpy as jnp
from jax import lax
from jax.experimental import pallas as pl
from jax.experimental.pallas import tpu as pltpu
from jax.sharding import PartitionSpec as P

WINDOW = 256
CHUNKS = 2
MESH = pl.DeviceIdType.MESH
F32 = jnp.float32
BF16 = jnp.bfloat16


def dot(a, b):
    return jnp.dot(a, b, preferred_element_type=F32)


def dot_t(a, b):
    return lax.dot_general(a, b, (((1,), (1,)), ((), ())), preferred_element_type=F32)


def silu_from_half(t):
    return t + t * jnp.tanh(t)


def kernel(
    n,
    cores,
    heads,
    x_hbm,
    w_hbm,
    cand_ref,
    table_ref,
    len_ref,
    bucket_ref,
    owner_ref,
    out_ref,
    cand_out_ref,
    x_v,
    w_v,
    q_v,
    k_v,
    v_v,
    xe,
    ke_v,
    ve_v,
    acc,
    aux,
    aux_e,
    cand_rows,
    q_send,
    q_recv,
    p_send,
    p_recv,
    load_sem,
    qs_sem,
    qr_sem,
    ps_sem,
    pr_sem,
    es_sem,
    er_sem,
    as_sem,
    ar_sem,
    fs_sem,
    fr_sem,
):
    group = lax.axis_index("groups")
    me = lax.axis_index("ctx")
    core = lax.axis_index("head")
    rows, width = x_v.shape
    part = q_v.shape[1]
    size = part // heads
    half_scale = 0.5 * size ** (-0.5)
    cands = cand_ref.shape[0]
    total = cands * n
    slot = cands * heads
    fold = max(1, 8 // cands)
    unroll = n <= 16

    def peers(body):
        if unroll:
            for step in range(1, n):
                body(step)
        else:
            lax.fori_loop(1, n, lambda step, carry: (body(step), carry)[1], 0)

    loads = [pltpu.make_async_copy(w_hbm.at[0], w_v.at[0], load_sem.at[0])]
    loads.append(pltpu.make_async_copy(x_hbm, x_v, load_sem.at[3]))
    loads.append(pltpu.make_async_copy(w_hbm.at[1], w_v.at[1], load_sem.at[1]))
    loads.append(pltpu.make_async_copy(w_hbm.at[2], w_v.at[2], load_sem.at[2]))
    for load in loads:
        load.start()

    barrier = pltpu.get_barrier_semaphore()

    def greet(step):
        pl.semaphore_signal(
            barrier,
            inc=1,
            device_id=(group, lax.rem(me + step, n), core),
            device_id_type=MESH,
        )

    peers(greet)
    for step in range(1, cores):
        pl.semaphore_signal(
            barrier,
            inc=1,
            device_id=(group, me, lax.rem(core + step, cores)),
            device_id_type=MESH,
        )

    buckets = table_ref.shape[0]
    hot = (
        lax.broadcasted_iota(jnp.int32, (buckets, rows), 0) == bucket_ref[...]
    ).astype(F32)
    bias = lax.dot_general(
        table_ref[...].astype(BF16),
        hot.astype(BF16),
        (((0,), (0,)), ((), ())),
        preferred_element_type=F32,
    )
    aux[...] = jnp.full(aux.shape, len_ref[0].astype(F32), F32)
    aux[pl.ds(0, heads), :] = 0.5 * bias

    for head in range(heads):
        cand_rows[pl.ds(head * cands, cands), :] = cand_ref[...].astype(F32)
    loads[0].wait()
    own = dot(cand_rows[...].astype(BF16), w_v[0])
    row_head = lax.broadcasted_iota(jnp.int32, (slot, size), 0) // cands
    picked = own[:, 0:size]
    for head in range(1, heads):
        picked = jnp.where(row_head == head, own[:, head * size : (head + 1) * size], picked)
    q_send[...] = picked.astype(BF16)
    own_slot = pl.ds(pl.multiple_of(me * slot, slot), slot)
    q_recv[own_slot, :] = picked.astype(BF16)

    pl.semaphore_wait(barrier, n - 1 + cores - 1)

    def query_copy(step):
        return pltpu.make_async_remote_copy(
            src_ref=q_send,
            dst_ref=q_recv.at[own_slot, :],
            send_sem=qs_sem.at[step],
            recv_sem=qr_sem.at[step],
            device_id=(group, lax.rem(me + step, n), core),
            device_id_type=MESH,
        )

    peers(lambda step: query_copy(step).start())

    chunk = rows // (cores * CHUNKS)

    def rows_of(owner_core, index):
        first = owner_core * (chunk * CHUNKS) + index * chunk
        return pl.ds(pl.multiple_of(first, chunk), chunk)

    def edge_copy(index):
        return pltpu.make_async_remote_copy(
            src_ref=x_hbm.at[rows_of(core, index), :],
            dst_ref=xe.at[rows_of(core, index), :],
            send_sem=es_sem.at[index],
            recv_sem=er_sem.at[index],
            device_id=(group, lax.rem(me + 1, n), core),
            device_id_type=MESH,
        )

    aux_copy = pltpu.make_async_remote_copy(
        src_ref=aux,
        dst_ref=aux_e,
        send_sem=as_sem,
        recv_sem=ar_sem,
        device_id=(group, lax.rem(me + 1, n), core),
        device_id_type=MESH,
    )

    def forward(step, index):
        return pltpu.make_async_remote_copy(
            src_ref=xe.at[rows_of(core, index), :],
            dst_ref=xe.at[rows_of(core, index), :],
            send_sem=fs_sem.at[step - 1, index],
            recv_sem=fr_sem.at[step - 1, index],
            device_id=(group, me, lax.rem(core + step, cores)),
            device_id_type=MESH,
        )

    @pl.when(me < n - 1)
    def _():
        aux_copy.start()
        for index in range(CHUNKS):
            edge_copy(index).start()

    loads[1].wait()
    loads[2].wait()
    k_v[...] = dot(x_v[...], w_v[1]).astype(BF16)
    loads[3].wait()
    valid = lax.broadcasted_iota(jnp.int32, (rows, part), 0) < len_ref[0]
    v_v[...] = jnp.where(valid, dot(x_v[...], w_v[2]), 0.0).astype(BF16)

    group_heads = heads // fold
    out_rows = n * fold * cands
    tall = lax.broadcasted_iota(jnp.int32, (out_rows, total), 0)
    place = (tall // (fold * cands)) * cands + lax.rem(tall, cands)
    sits = (owner_ref[...] == place).astype(F32).astype(BF16)
    lane = lax.broadcasted_iota(jnp.int32, (total, n * slot), 1)
    source = (lane // slot) * cands + lax.rem(lane, cands)
    spread = (lax.broadcasted_iota(jnp.int32, (total, n * slot), 0) == source).astype(F32)
    chosen = dot(sits, spread.astype(BF16))
    lane_head = lax.rem(
        lax.broadcasted_iota(jnp.int32, (out_rows, n * slot), 1) // cands, heads
    )
    row_fold = lax.rem(
        lax.broadcasted_iota(jnp.int32, (out_rows, n * slot), 0) // cands, fold
    )
    peers(lambda step: query_copy(step).wait_recv())
    norm = (rows * n) ** (-0.5)

    def folded(parts, shape):
        fold_of = lax.rem(lax.broadcasted_iota(jnp.int32, shape, 0) // cands, fold)
        value = parts[0]
        for index in range(1, fold):
            value = jnp.where(fold_of == index, parts[index], value)
        return value

    for column in range(group_heads):
        select = jnp.where(lane_head == row_fold * group_heads + column, chosen, 0.0)
        query = dot(select.astype(BF16), q_recv[...]).astype(BF16)
        heads_here = [f * group_heads + column for f in range(fold)]
        spans = [slice(h * size, (h + 1) * size) for h in heads_here]
        t = folded(
            [
                dot_t(query, k_v[:, span]) * half_scale + aux[pl.ds(h, 1), :]
                for h, span in zip(heads_here, spans)
            ],
            (out_rows, rows),
        )
        weight = silu_from_half(t).astype(BF16)
        p_send[:, column * size : (column + 1) * size] = norm * folded(
            [dot(weight, v_v[:, span]) for span in spans], (out_rows, size)
        )
    tile = fold * cands
    own_tile = pl.ds(pl.multiple_of(me * tile, tile), tile)

    def partial_copy(step):
        to = lax.rem(me + step, n)
        return pltpu.make_async_remote_copy(
            src_ref=p_send.at[pl.ds(pl.multiple_of(to * tile, tile), tile), :],
            dst_ref=p_recv.at[own_tile, :],
            send_sem=ps_sem.at[step],
            recv_sem=pr_sem.at[step],
            device_id=(group, to, core),
            device_id_type=MESH,
        )

    peers(lambda step: partial_copy(step).start())
    p_recv[own_tile, :] = p_send[own_tile, :]

    q_v[...] = dot(x_v[...], w_v[0]).astype(BF16)
    below = lax.broadcasted_iota(jnp.int32, (rows, rows), 0) >= lax.broadcasted_iota(
        jnp.int32, (rows, rows), 1
    )
    for head in range(heads):
        span = slice(head * size, (head + 1) * size)
        t = dot_t(q_v[:, span], k_v[:, span]) * half_scale + aux[pl.ds(head, 1), :]
        weight = jnp.where(below, silu_from_half(t), 0.0).astype(BF16)
        acc[:, span] = dot(weight, v_v[:, span])

    out_scale = WINDOW ** (-0.5)

    @pl.when(me == 0)
    def _():
        out_ref[...] = jnp.where(valid, acc[...] * out_scale, 0.0).astype(BF16)

    @pl.when(me > 0)
    def _():
        for index in range(CHUNKS):
            edge_copy(index).wait_recv()
            for step in range(1, cores):
                forward(step, index).start()
        aux_copy.wait_recv()
        for step in range(1, cores):
            for index in range(CHUNKS):
                forward(step, index).wait_recv()
        ke_v[...] = dot(xe[...], w_v[1]).astype(BF16)
        edge_valid = (
            lax.broadcasted_iota(jnp.int32, (rows, part), 0).astype(F32) < aux_e[heads, 0]
        )
        ve_v[...] = jnp.where(edge_valid, dot(xe[...], w_v[2]), 0.0).astype(BF16)
        for head in range(heads):
            span = slice(head * size, (head + 1) * size)
            t = dot_t(q_v[:, span], ke_v[:, span]) * half_scale + aux_e[pl.ds(head, 1), :]
            weight = jnp.where(below, 0.0, silu_from_half(t)).astype(BF16)
            value = (acc[:, span] + dot(weight, ve_v[:, span])) * out_scale
            out_ref[:, span] = jnp.where(valid[:, span], value, 0.0).astype(BF16)
        for step in range(1, cores):
            for index in range(CHUNKS):
                forward(step, index).wait_send()

    peers(lambda step: partial_copy(step).wait_recv())
    if unroll:
        summed = p_recv[pl.ds(0, tile), :]
        for index in range(1, n):
            summed = summed + p_recv[pl.ds(index * tile, tile), :]
    else:
        summed = lax.fori_loop(
            0,
            n,
            lambda i, s: s + p_recv[pl.ds(pl.multiple_of(i * tile, tile), tile), :],
            jnp.zeros((tile, p_recv.shape[1]), F32),
        )
    group_width = group_heads * size
    for index in range(fold):
        cand_out_ref[:, index * group_width : (index + 1) * group_width] = summed[
            index * cands : (index + 1) * cands, :
        ].astype(BF16)

    peers(lambda step: query_copy(step).wait_send())
    peers(lambda step: partial_copy(step).wait_send())

    @pl.when(me < n - 1)
    def _():
        aux_copy.wait_send()
        for index in range(CHUNKS):
            edge_copy(index).wait_send()


def local(n, cores, hist_x, cand_x, w_qkv, rab_table, hist_len, hist_bucket, cand_owner):
    rows, width = hist_x.shape
    part = w_qkv.shape[2]
    heads = rab_table.shape[1]
    size = part // heads
    cands = cand_x.shape[0]
    slot = cands * heads
    fold = max(1, 8 // cands)
    tile = fold * cands
    dma = pltpu.SemaphoreType.DMA
    vmem = pl.BlockSpec(memory_space=pltpu.VMEM)
    hbm = pl.BlockSpec(memory_space=pltpu.HBM)
    smem = pl.BlockSpec(memory_space=pltpu.SMEM)
    return pl.pallas_call(
        functools.partial(kernel, n, cores, heads),
        out_shape=(
            jax.ShapeDtypeStruct((rows, part), BF16),
            jax.ShapeDtypeStruct((cands, part), BF16),
        ),
        in_specs=[hbm, hbm, vmem, vmem, smem, vmem, vmem],
        out_specs=(vmem, vmem),
        scratch_shapes=[
            pltpu.VMEM((rows, width), BF16),
            pltpu.VMEM(w_qkv.shape, BF16),
            pltpu.VMEM((rows, part), BF16),
            pltpu.VMEM((rows, part), BF16),
            pltpu.VMEM((rows, part), BF16),
            pltpu.VMEM((rows, width), BF16),
            pltpu.VMEM((rows, part), BF16),
            pltpu.VMEM((rows, part), BF16),
            pltpu.VMEM((rows, part), F32),
            pltpu.VMEM((8, rows), F32),
            pltpu.VMEM((8, rows), F32),
            pltpu.VMEM((slot, width), F32),
            pltpu.VMEM((slot, size), BF16),
            pltpu.VMEM((n * slot, size), BF16),
            pltpu.VMEM((n * tile, part // fold), F32),
            pltpu.VMEM((n * tile, part // fold), F32),
            dma((4,)),
            dma((n,)),
            dma((n,)),
            dma((n,)),
            dma((n,)),
            dma((CHUNKS,)),
            dma((CHUNKS,)),
            dma,
            dma,
            dma((max(cores - 1, 1), CHUNKS)),
            dma((max(cores - 1, 1), CHUNKS)),
        ],
        compiler_params=pltpu.CompilerParams(
            collective_id=0,
            has_side_effects=True,
            vmem_limit_bytes=48 * 1024 * 1024,
        ),
    )(
        hist_x,
        w_qkv,
        cand_x,
        rab_table,
        hist_len,
        hist_bucket.reshape(1, rows),
        cand_owner.reshape(1, cands * n),
    )


def solution(mesh):
    placed = (
        P(("groups", "ctx"), None),
        P(("groups", "ctx"), None),
        P(None, None, "head"),
        P(None, "head"),
        P(("groups", "ctx")),
        P(("groups", "ctx")),
        P("groups"),
    )
    return jax.shard_map(
        functools.partial(local, mesh.shape["ctx"], mesh.shape["head"]),
        mesh=mesh,
        in_specs=placed,
        out_specs=(P(("groups", "ctx"), "head"), P(("groups", "ctx"), "head")),
        check_vma=False,
    )
```

time: 92.6 us -> 24.4 us (0.26)
  blocking collectives: 65.2 us -> 0 us
  Pallas kernels: 0 us -> 15.6 us
  starting transfers between devices: 11.9 us -> 0 us
  matrix products: 8.81 us -> 0 us
  local copies, waits for them, and re-layouts: 3.02 us -> 7.04 us
  other arithmetic: 1.08 us -> 0 us
    unnamed x1 -> x0, blocking collectives: 34.8 us -> none
    all_gather x1 -> x0, blocking collectives: 30.4 us -> none  [local(): all_query = lax.all_gather(own_query, 'ctx', axis=0, tiled=True)]
    pallas_call x0 -> x1, Pallas kernels: none -> 15.6 us  [local(): pl.pallas_call(functools.partial(kernel, n, cores, heads), out_shape=(jax...]
    ppermute x3 -> x0, starting transfers between devices: 11.9 us -> none  [from_behind(): lax.ppermute(value, axis, [(source, source + steps) for source in range(l...]
    dot_general x7 -> x0, matrix products: 8.81 us -> none  [the longest x1 1.66 us: local(): jnp.dot(hist_x, w_qkv[2], preferred_element_type=jnp.float32)]
    unnamed x10 -> x13, local copies, waits for them, and re-layouts: 0.62 us -> 7.04 us
  transfers between devices with their start and end apart: 3 -> 0, of which waited for: 0 -> 0; matrix products, arithmetic and copies ran while one was open for 11% -> 0% of each run, Pallas kernels for 0% -> 0%
where the time goes in v1:
time: 24.4 us; the launch traced here: 24 us
  Pallas kernels  15.6 us (64%)
  local copies, waits for them, and re-layouts  7.04 us (29%)
  between operations  1.3 us (5%)
    pallas_call x1, Pallas kernels, local(): pl.pallas_call(functools.partial(kernel, n, cores, heads), out_shape=(jax...  15.6 us
    unnamed x13, local copies, waits for them, and re-layouts  7.04 us

profile of v1, /device:TPU:0, one launch (start us, length us, event | category | flops | bytes accessed | tf_op | source)
XLA Modules:
  0.0 24.0 jit_solution(421577421709271640)
XLA Ops:
  1.3 0.8 %copy.9.table_ref = f32[128,4]{1,0:T(8,128)S(1)} copy(f32[128,4]{0,1:T(4,128)} %param.10) | data formatting | bytes 4096 | tf_op args[3]
  2.1 0.0 copy-start
  2.1 1.9 %copy-done = bf16[3,1024,512]{2,1,0:T(8,128)(2,1)S(1)} copy-done((bf16[3,1024,512]{2,1,0:T(8,128)(2,1)S(1)}, bf16[3,1024,512]{2,1,0:T(8,128)(2,1)}, u32[]{:S(2)}) %copy-start) | copy-done | bytes 3145752
  4.0 0.0 copy-start.1
  4.0 1.0 %copy-done.1 = bf16[256,1024]{1,0:T(8,128)(2,1)S(1)} copy-done((bf16[256,1024]{1,0:T(8,128)(2,1)S(1)}, bf16[256,1024]{1,0:T(8,128)(2,1)}, u32[]{:S(2)}) %copy-start.1) | copy-done | bytes 524312
  5.0 0.0 copy-start.2
  5.0 0.7 %copy-done.2 = bf16[4,1024]{1,0:T(4,128)(2,1)S(1)} copy-done((bf16[4,1024]{1,0:T(4,128)(2,1)S(1)}, bf16[4,1024]{1,0:T(4,128)(2,1)}, u32[]{:S(2)}) %copy-start.2) | copy-done | bytes 8216
  5.7 0.0 copy-start.3
  5.7 0.7 %copy-done.3 = s32[256]{0:T(256)S(1)} copy-done((s32[256]{0:T(256)S(1)}, s32[256]{0:T(256)}, u32[]{:S(2)}) %copy-start.3) | copy-done | bytes 1048
  6.4 0.0 copy-start.4
  6.4 0.7 %copy-done.4 = s32[32]{0:T(128)S(1)} copy-done((s32[32]{0:T(128)S(1)}, s32[32]{0:T(128)}, u32[]{:S(2)}) %copy-start.4) | copy-done | bytes 152
  7.0 15.6 %shard_map.86 = (bf16[256,512]{1,0:T(8,128)(2,1)S(1)}, bf16[4,512]{1,0:T(4,128)(2,1)S(1)}) custom-call(bf16[256,1024]{1,0:T(8,128)(2,1)S(1)} %copy-done.1, bf16[3,1024,512]{2,1,0:T(8,128)(2,1)S(1)} %copy-done, bf16[4,1024]{1,0:T(4,128)(2,1)S(1)} %copy-done.2, f32[128,4]{1,0:T(8,128)S(1)} %copy.9.table_ref, s32[1]{0:T(128)S(6)} %copy.12.len_ref, ...), custom_call_target="tpu_custom_call" | custom-call | tf_op jit(solution)/shard_map/pallas_call | solution.py:343
  22.7 0.7 %copy.13 = bf16[256,512]{1,0:T(8,128)(2,1)} copy(bf16[256,512]{1,0:T(8,128)(2,1)S(1)} %get-tuple-element.4) | data formatting | bytes 524288
  23.4 0.6 %copy.14 = bf16[4,512]{1,0:T(4,128)(2,1)} copy(bf16[4,512]{1,0:T(4,128)(2,1)S(1)} %get-tuple-element.5) | data formatting | bytes 8192
Async XLA Ops:
  2.1 1.9 %copy-start = (bf16[3,1024,512]{2,1,0:T(8,128)(2,1)S(1)}, bf16[3,1024,512]{2,1,0:T(8,128)(2,1)}, u32[]{:S(2)}) copy-start(bf16[3,1024,512]{2,1,0:T(8,128)(2,1)} %w_hbm.1) | copy-start | bytes 9437188
  4.0 1.0 %copy-start.1 = (bf16[256,1024]{1,0:T(8,128)(2,1)S(1)}, bf16[256,1024]{1,0:T(8,128)(2,1)}, u32[]{:S(2)}) copy-start(bf16[256,1024]{1,0:T(8,128)(2,1)} %x_hbm.1) | copy-start | bytes 1572868
  5.0 0.7 %copy-start.2 = (bf16[4,1024]{1,0:T(4,128)(2,1)S(1)}, bf16[4,1024]{1,0:T(4,128)(2,1)}, u32[]{:S(2)}) copy-start(bf16[4,1024]{1,0:T(4,128)(2,1)} %cand_ref.1) | copy-start | bytes 24580
  5.7 0.7 %copy-start.3 = (s32[256]{0:T(256)S(1)}, s32[256]{0:T(256)}, u32[]{:S(2)}) copy-start(s32[256]{0:T(256)} %param.12) | copy-start | bytes 3076
  6.4 0.7 %copy-start.4 = (s32[32]{0:T(128)S(1)}, s32[32]{0:T(128)}, u32[]{:S(2)}) copy-start(s32[32]{0:T(128)} %param.13) | copy-start | bytes 388

commit v2 on v1

--- a/solution.py
+++ b/solution.py
@@ -9,6 +9,7 @@
 
 WINDOW = 256
 CHUNKS = 2
+VMEM_LIMIT = 63 * 1024 * 1024
 MESH = pl.DeviceIdType.MESH
 F32 = jnp.float32
 BF16 = jnp.bfloat16
@@ -32,13 +33,18 @@
     heads,
     x_hbm,
     w_hbm,
+    cand_hbm,
+    table_hbm,
+    len_hbm,
+    bucket_hbm,
+    owner_hbm,
+    out_ref,
+    cand_out_ref,
     cand_ref,
     table_ref,
     len_ref,
     bucket_ref,
     owner_ref,
-    out_ref,
-    cand_out_ref,
     x_v,
     w_v,
     q_v,
@@ -87,10 +93,21 @@
         else:
             lax.fori_loop(1, n, lambda step, carry: (body(step), carry)[1], 0)
 
-    loads = [pltpu.make_async_copy(w_hbm.at[0], w_v.at[0], load_sem.at[0])]
-    loads.append(pltpu.make_async_copy(x_hbm, x_v, load_sem.at[3]))
-    loads.append(pltpu.make_async_copy(w_hbm.at[1], w_v.at[1], load_sem.at[1]))
-    loads.append(pltpu.make_async_copy(w_hbm.at[2], w_v.at[2], load_sem.at[2]))
+    pairs = [
+        (cand_hbm, cand_ref),
+        (len_hbm, len_ref),
+        (bucket_hbm, bucket_ref),
+        (table_hbm, table_ref),
+        (owner_hbm, owner_ref),
+        (w_hbm.at[0], w_v.at[0]),
+        (x_hbm, x_v),
+        (w_hbm.at[1], w_v.at[1]),
+        (w_hbm.at[2], w_v.at[2]),
+    ]
+    loads = [
+        pltpu.make_async_copy(source, target, load_sem.at[index])
+        for index, (source, target) in enumerate(pairs)
+    ]
     for load in loads:
         load.start()
 
@@ -113,14 +130,17 @@
             device_id_type=MESH,
         )
 
-    buckets = table_ref.shape[0]
+    for load in loads[:5]:
+        load.wait()
+
+    buckets = table_ref.shape[1]
     hot = (
         lax.broadcasted_iota(jnp.int32, (buckets, rows), 0) == bucket_ref[...]
     ).astype(F32)
     bias = lax.dot_general(
         table_ref[...].astype(BF16),
         hot.astype(BF16),
-        (((0,), (0,)), ((), ())),
+        (((1,), (0,)), ((), ())),
         preferred_element_type=F32,
     )
     aux[...] = jnp.full(aux.shape, len_ref[0].astype(F32), F32)
@@ -128,7 +148,7 @@
 
     for head in range(heads):
         cand_rows[pl.ds(head * cands, cands), :] = cand_ref[...].astype(F32)
-    loads[0].wait()
+    loads[5].wait()
     own = dot(cand_rows[...].astype(BF16), w_v[0])
     row_head = lax.broadcasted_iota(jnp.int32, (slot, size), 0) // cands
     picked = own[:, 0:size]
@@ -193,10 +213,10 @@
         for index in range(CHUNKS):
             edge_copy(index).start()
 
-    loads[1].wait()
-    loads[2].wait()
+    loads[6].wait()
+    loads[7].wait()
     k_v[...] = dot(x_v[...], w_v[1]).astype(BF16)
-    loads[3].wait()
+    loads[8].wait()
     valid = lax.broadcasted_iota(jnp.int32, (rows, part), 0) < len_ref[0]
     v_v[...] = jnp.where(valid, dot(x_v[...], w_v[2]), 0.0).astype(BF16)
 
@@ -339,16 +359,20 @@
     dma = pltpu.SemaphoreType.DMA
     vmem = pl.BlockSpec(memory_space=pltpu.VMEM)
     hbm = pl.BlockSpec(memory_space=pltpu.HBM)
-    smem = pl.BlockSpec(memory_space=pltpu.SMEM)
     return pl.pallas_call(
         functools.partial(kernel, n, cores, heads),
         out_shape=(
             jax.ShapeDtypeStruct((rows, part), BF16),
             jax.ShapeDtypeStruct((cands, part), BF16),
         ),
-        in_specs=[hbm, hbm, vmem, vmem, smem, vmem, vmem],
+        in_specs=[hbm] * 7,
         out_specs=(vmem, vmem),
         scratch_shapes=[
+            pltpu.VMEM(cand_x.shape, BF16),
+            pltpu.VMEM(rab_table.shape[::-1], F32),
+            pltpu.SMEM(hist_len.shape, jnp.int32),
+            pltpu.VMEM((1, rows), jnp.int32),
+            pltpu.VMEM((1, cands * n), jnp.int32),
             pltpu.VMEM((rows, width), BF16),
             pltpu.VMEM(w_qkv.shape, BF16),
             pltpu.VMEM((rows, part), BF16),
@@ -365,7 +389,7 @@
             pltpu.VMEM((n * slot, size), BF16),
             pltpu.VMEM((n * tile, part // fold), F32),
             pltpu.VMEM((n * tile, part // fold), F32),
-            dma((4,)),
+            dma((9,)),
             dma((n,)),
             dma((n,)),
             dma((n,)),
@@ -380,13 +404,13 @@
         compiler_params=pltpu.CompilerParams(
             collective_id=0,
             has_side_effects=True,
-            vmem_limit_bytes=48 * 1024 * 1024,
+            vmem_limit_bytes=VMEM_LIMIT,
         ),
     )(
         hist_x,
         w_qkv,
         cand_x,
-        rab_table,
+        rab_table.T,
         hist_len,
         hist_bucket.reshape(1, rows),
         cand_owner.reshape(1, cands * n),

time: 24.4 us -> 20.7 us (0.85)
  local copies, waits for them, and re-layouts: 7.04 us -> 2.95 us
  Pallas kernels: 15.6 us -> 16.2 us
    unnamed x13 -> x2, local copies, waits for them, and re-layouts: 7.04 us -> 2.95 us
    pallas_call x1, Pallas kernels: 15.6 us -> 16.2 us  [local(): pl.pallas_call(functools.partial(kernel, n, cores, heads), out_shape=(jax...]
where the time goes in v2:
time: 20.7 us; the launch traced here: 20.4 us
  Pallas kernels  16.2 us (78%)
  local copies, waits for them, and re-layouts  2.95 us (14%)
  between operations  1.29 us (6%)
    pallas_call x1, Pallas kernels, local(): pl.pallas_call(functools.partial(kernel, n, cores, heads), out_shape=(jax...  16.2 us
    unnamed x2, local copies, waits for them, and re-layouts  2.95 us

profile of v2, /device:TPU:0, one launch (start us, length us, event | category | flops | bytes accessed | tf_op | source)
XLA Modules:
  0.0 20.4 jit_solution(2250684803509608831)
XLA Ops:
  1.3 16.2 %shard_map.86 = (bf16[256,512]{1,0:T(8,128)(2,1)}, bf16[4,512]{1,0:T(4,128)(2,1)}) custom-call(bf16[256,1024]{1,0:T(8,128)(2,1)} %x_hbm.1, bf16[3,1024,512]{2,1,0:T(8,128)(2,1)} %w_hbm.1, bf16[4,1024]{1,0:T(4,128)(2,1)} %cand_hbm.1, f32[4,128]{1,0:T(4,128)} %bitcast.3, s32[1]{0:T(128)S(6)} %copy.11.len_hbm, s32[1,256]{1,0:T(1,128)} %bitcast.4, s32[1,32]{1,0:T(1,128)} %bitcast.5), custom_call_target="tpu_custom_call" | custom-call | tf_op jit(solution)/shard_map/pallas_call | solution.py:362
  17.5 1.7 %copy.12 = bf16[256,512]{1,0:T(8,128)(2,1)} copy(bf16[256,512]{1,0:T(8,128)(2,1)} %get-tuple-element.4) | data formatting | bytes 524288
  19.1 1.3 %copy.13 = bf16[4,512]{1,0:T(4,128)(2,1)} copy(bf16[4,512]{1,0:T(4,128)(2,1)} %get-tuple-element.5) | data formatting | bytes 8192

commit v3 on v2

--- a/solution.py
+++ b/solution.py
@@ -9,7 +9,7 @@
 
 WINDOW = 256
 CHUNKS = 2
-VMEM_LIMIT = 63 * 1024 * 1024
+VMEM_LIMIT = 48 * 1024 * 1024
 MESH = pl.DeviceIdType.MESH
 F32 = jnp.float32
 BF16 = jnp.bfloat16
@@ -35,9 +35,9 @@
     w_hbm,
     cand_hbm,
     table_hbm,
-    len_hbm,
     bucket_hbm,
     owner_hbm,
+    len_hbm,
     out_ref,
     cand_out_ref,
     cand_ref,
@@ -51,8 +51,6 @@
     k_v,
     v_v,
     xe,
-    ke_v,
-    ve_v,
     acc,
     aux,
     aux_e,
@@ -133,6 +131,7 @@
     for load in loads[:5]:
         load.wait()
 
+    length = len_ref[0, 0]
     buckets = table_ref.shape[1]
     hot = (
         lax.broadcasted_iota(jnp.int32, (buckets, rows), 0) == bucket_ref[...]
@@ -143,7 +142,7 @@
         (((1,), (0,)), ((), ())),
         preferred_element_type=F32,
     )
-    aux[...] = jnp.full(aux.shape, len_ref[0].astype(F32), F32)
+    aux[...] = jnp.full(aux.shape, length.astype(F32), F32)
     aux[pl.ds(0, heads), :] = 0.5 * bias
 
     for head in range(heads):
@@ -158,6 +157,13 @@
     own_slot = pl.ds(pl.multiple_of(me * slot, slot), slot)
     q_recv[own_slot, :] = picked.astype(BF16)
 
+    loads[6].wait()
+    loads[7].wait()
+    k_v[...] = dot(x_v[...], w_v[1]).astype(BF16)
+    loads[8].wait()
+    valid = lax.broadcasted_iota(jnp.int32, (rows, part), 0) < length
+    v_v[...] = jnp.where(valid, dot(x_v[...], w_v[2]), 0.0).astype(BF16)
+
     pl.semaphore_wait(barrier, n - 1 + cores - 1)
 
     def query_copy(step):
@@ -212,13 +218,6 @@
         aux_copy.start()
         for index in range(CHUNKS):
             edge_copy(index).start()
-
-    loads[6].wait()
-    loads[7].wait()
-    k_v[...] = dot(x_v[...], w_v[1]).astype(BF16)
-    loads[8].wait()
-    valid = lax.broadcasted_iota(jnp.int32, (rows, part), 0) < len_ref[0]
-    v_v[...] = jnp.where(valid, dot(x_v[...], w_v[2]), 0.0).astype(BF16)
 
     group_heads = heads // fold
     out_rows = n * fold * cands
@@ -301,20 +300,36 @@
             for step in range(1, cores):
                 forward(step, index).start()
         aux_copy.wait_recv()
-        for step in range(1, cores):
-            for index in range(CHUNKS):
-                forward(step, index).wait_recv()
-        ke_v[...] = dot(xe[...], w_v[1]).astype(BF16)
-        edge_valid = (
-            lax.broadcasted_iota(jnp.int32, (rows, part), 0).astype(F32) < aux_e[heads, 0]
-        )
-        ve_v[...] = jnp.where(edge_valid, dot(xe[...], w_v[2]), 0.0).astype(BF16)
-        for head in range(heads):
-            span = slice(head * size, (head + 1) * size)
-            t = dot_t(q_v[:, span], ke_v[:, span]) * half_scale + aux_e[pl.ds(head, 1), :]
-            weight = jnp.where(below, 0.0, silu_from_half(t)).astype(BF16)
-            value = (acc[:, span] + dot(weight, ve_v[:, span])) * out_scale
-            out_ref[:, span] = jnp.where(valid[:, span], value, 0.0).astype(BF16)
+        half = rows // cores
+        for step in range(cores):
+            if step > 0:
+                for index in range(CHUNKS):
+                    forward(step, index).wait_recv()
+            first = pl.multiple_of(lax.rem(core - step + cores, cores) * half, half)
+            piece = pl.ds(first, half)
+            edge_x = xe[piece, :]
+            edge_keys = dot(edge_x, w_v[1]).astype(BF16)
+            place = first + lax.broadcasted_iota(jnp.int32, (half, part), 0)
+            edge_values = jnp.where(
+                place.astype(F32) < aux_e[heads, 0], dot(edge_x, w_v[2]), 0.0
+            ).astype(BF16)
+            ahead = first + lax.broadcasted_iota(
+                jnp.int32, (rows, half), 1
+            ) > lax.broadcasted_iota(jnp.int32, (rows, half), 0)
+            for head in range(heads):
+                span = slice(head * size, (head + 1) * size)
+                t = (
+                    dot_t(q_v[:, span], edge_keys[:, span]) * half_scale
+                    + aux_e[pl.ds(head, 1), piece]
+                )
+                weight = jnp.where(ahead, silu_from_half(t), 0.0).astype(BF16)
+                value = acc[:, span] + dot(weight, edge_values[:, span])
+                if step < cores - 1:
+                    acc[:, span] = value
+                else:
+                    out_ref[:, span] = jnp.where(
+                        valid[:, span], value * out_scale, 0.0
+                    ).astype(BF16)
         for step in range(1, cores):
             for index in range(CHUNKS):
                 forward(step, index).wait_send()
@@ -362,15 +377,15 @@
     return pl.pallas_call(
         functools.partial(kernel, n, cores, heads),
         out_shape=(
-            jax.ShapeDtypeStruct((rows, part), BF16),
-            jax.ShapeDtypeStruct((cands, part), BF16),
+            pltpu.VMEM((rows, part), BF16),
+            pltpu.VMEM((cands, part), BF16),
         ),
         in_specs=[hbm] * 7,
         out_specs=(vmem, vmem),
         scratch_shapes=[
             pltpu.VMEM(cand_x.shape, BF16),
             pltpu.VMEM(rab_table.shape[::-1], F32),
-            pltpu.SMEM(hist_len.shape, jnp.int32),
+            pltpu.VMEM((1, 1), jnp.int32),
             pltpu.VMEM((1, rows), jnp.int32),
             pltpu.VMEM((1, cands * n), jnp.int32),
             pltpu.VMEM((rows, width), BF16),
@@ -379,8 +394,6 @@
             pltpu.VMEM((rows, part), BF16),
             pltpu.VMEM((rows, part), BF16),
             pltpu.VMEM((rows, width), BF16),
-            pltpu.VMEM((rows, part), BF16),
-            pltpu.VMEM((rows, part), BF16),
             pltpu.VMEM((rows, part), F32),
             pltpu.VMEM((8, rows), F32),
             pltpu.VMEM((8, rows), F32),
@@ -407,13 +420,18 @@
             vmem_limit_bytes=VMEM_LIMIT,
         ),
     )(
-        hist_x,
-        w_qkv,
-        cand_x,
-        rab_table.T,
-        hist_len,
-        hist_bucket.reshape(1, rows),
-        cand_owner.reshape(1, cands * n),
+        *(
+            pltpu.with_memory_space_constraint(operand, pltpu.HBM)
+            for operand in (
+                hist_x,
+                w_qkv,
+                cand_x,
+                rab_table.T,
+                hist_bucket.reshape(1, rows),
+                cand_owner.reshape(1, cands * n),
+            )
+        ),
+        hist_len.reshape(1, 1),
     )
 
 

time: 20.7 us -> 18.3 us (0.88)
  local copies, waits for them, and re-layouts: 2.95 us -> 1.3 us
  Pallas kernels: 16.2 us -> 15.5 us
    unnamed x2, local copies, waits for them, and re-layouts: 2.95 us -> 1.3 us
    pallas_call x1, Pallas kernels: 16.2 us -> 15.5 us  [local(): pl.pallas_call(functools.partial(kernel, n, cores, heads), out_shape=(plt...]
where the time goes in v3:
time: 18.3 us; the launch traced here: 18.1 us
  Pallas kernels  15.5 us (85%)
  local copies, waits for them, and re-layouts  1.3 us (7%)
  between operations  1.29 us (7%)
    pallas_call x1, Pallas kernels, local(): pl.pallas_call(functools.partial(kernel, n, cores, heads), out_shape=(plt...  15.5 us
    unnamed x2, local copies, waits for them, and re-layouts  1.3 us

profile of v3, /device:TPU:0, one launch (start us, length us, event | category | flops | bytes accessed | tf_op | source)
XLA Modules:
  0.0 18.1 jit_solution(10838287606819919818)
XLA Ops:
  1.3 15.5 %shard_map.86 = (bf16[256,512]{1,0:T(8,128)(2,1)S(1)}, bf16[4,512]{1,0:T(4,128)(2,1)S(1)}) custom-call(bf16[256,1024]{1,0:T(8,128)(2,1)} %x_hbm.1, bf16[3,1024,512]{2,1,0:T(8,128)(2,1)} %w_hbm.1, bf16[4,1024]{1,0:T(4,128)(2,1)} %cand_hbm.1, f32[4,128]{1,0:T(4,128)} %bitcast.5, s32[1,256]{1,0:T(1,128)} %bitcast.6, s32[1,32]{1,0:T(1,128)} %bitcast.7, ...), custom_call_target="tpu_custom_call" | custom-call | tf_op jit(solution)/shard_map/pallas_call | solution.py:377
  16.8 0.7 %copy.11 = bf16[256,512]{1,0:T(8,128)(2,1)} copy(bf16[256,512]{1,0:T(8,128)(2,1)S(1)} %get-tuple-element.2) | data formatting | bytes 524288
  17.5 0.6 %copy.12 = bf16[4,512]{1,0:T(4,128)(2,1)} copy(bf16[4,512]{1,0:T(4,128)(2,1)S(1)} %get-tuple-element.3) | data formatting | bytes 8192

commit v4 on v3

--- a/solution.py
+++ b/solution.py
@@ -86,10 +86,29 @@
 
     def peers(body):
         if unroll:
-            for step in range(1, n):
+            for step in sorted(range(1, n), key=lambda s: -abs(2 * s - n)):
                 body(step)
         else:
             lax.fori_loop(1, n, lambda step, carry: (body(step), carry)[1], 0)
+
+    barrier = pltpu.get_barrier_semaphore()
+
+    def greet(step):
+        pl.semaphore_signal(
+            barrier,
+            inc=1,
+            device_id=(group, lax.rem(me + step, n), core),
+            device_id_type=MESH,
+        )
+
+    peers(greet)
+    for step in range(1, cores):
+        pl.semaphore_signal(
+            barrier,
+            inc=1,
+            device_id=(group, me, lax.rem(core + step, cores)),
+            device_id_type=MESH,
+        )
 
     pairs = [
         (cand_hbm, cand_ref),
@@ -108,25 +127,6 @@
     ]
     for load in loads:
         load.start()
-
-    barrier = pltpu.get_barrier_semaphore()
-
-    def greet(step):
-        pl.semaphore_signal(
-            barrier,
-            inc=1,
-            device_id=(group, lax.rem(me + step, n), core),
-            device_id_type=MESH,
-        )
-
-    peers(greet)
-    for step in range(1, cores):
-        pl.semaphore_signal(
-            barrier,
-            inc=1,
-            device_id=(group, me, lax.rem(core + step, cores)),
-            device_id_type=MESH,
-        )
 
     for load in loads[:5]:
         load.wait()

time: 18.3 us -> 18.1 us (0.989)
  Pallas kernels: 15.5 us -> 15.3 us
    pallas_call x1, Pallas kernels: 15.5 us -> 15.3 us  [local(): pl.pallas_call(functools.partial(kernel, n, cores, heads), out_shape=(plt...]
where the time goes in v4:
time: 18.1 us; the launch traced here: 17.9 us
  Pallas kernels  15.3 us (85%)
  local copies, waits for them, and re-layouts  1.3 us (7%)
  between operations  1.29 us (7%)
    pallas_call x1, Pallas kernels, local(): pl.pallas_call(functools.partial(kernel, n, cores, heads), out_shape=(plt...  15.3 us
    unnamed x2, local copies, waits for them, and re-layouts  1.3 us

profile of v4, /device:TPU:0, one launch (start us, length us, event | category | flops | bytes accessed | tf_op | source)
XLA Modules:
  0.0 17.9 jit_solution(7769895108375149229)
XLA Ops:
  1.3 15.3 %shard_map.86 = (bf16[256,512]{1,0:T(8,128)(2,1)S(1)}, bf16[4,512]{1,0:T(4,128)(2,1)S(1)}) custom-call(bf16[256,1024]{1,0:T(8,128)(2,1)} %x_hbm.1, bf16[3,1024,512]{2,1,0:T(8,128)(2,1)} %w_hbm.1, bf16[4,1024]{1,0:T(4,128)(2,1)} %cand_hbm.1, f32[4,128]{1,0:T(4,128)} %bitcast.5, s32[1,256]{1,0:T(1,128)} %bitcast.6, s32[1,32]{1,0:T(1,128)} %bitcast.7, ...), custom_call_target="tpu_custom_call" | custom-call | tf_op jit(solution)/shard_map/pallas_call | solution.py:377
  16.6 0.7 %copy.11 = bf16[256,512]{1,0:T(8,128)(2,1)} copy(bf16[256,512]{1,0:T(8,128)(2,1)S(1)} %get-tuple-element.2) | data formatting | bytes 524288
  17.3 0.6 %copy.12 = bf16[4,512]{1,0:T(4,128)(2,1)} copy(bf16[4,512]{1,0:T(4,128)(2,1)S(1)} %get-tuple-element.3) | data formatting | bytes 8192
